TPU v7x, 32 devices: a whole 2x2x4 slice. The times are simulated.
32 devices in a mesh: wide: 8 (over z, y), narrow: 4 (over x, core).
Axes of the slice: x: 2, y: 2, z: 4, core: 2. Of those that a mesh axis runs over, the one named last changes fastest.
Arguments:
- control: bfloat16 [512, 2, 512, 512], P('wide', None, None, 'narrow'), may hold values from -6 to 6
- legendre: bfloat16 [512, 512, 512], P('wide'), may hold values from -0.25 to 0.25
- loc_spectrum: float32 [512, 512], P('wide'), may hold values from 0.02 to 0.2
- ensemble: bfloat16 [512, 512, 1024], P('wide', 'narrow'), may hold values from -0.29882812 to 0.29882812
- order_map: int32 [512], replicated, may hold values from 0 to 511, each once
- obs_level: int32 [512, 256], P('wide'), may hold values from 0 to 7
- obs_lon: int32 [512, 256], P('wide'), may hold values from 0 to 1023
- obs_value: float32 [512, 256], P('wide'), may hold values from -12 to 12
- obs_weight: float32 [512, 256], P('wide'), may hold values from 2 to 40
Outputs:
- gradient: float32 [512, 2, 512, 512], P('wide', None, None, 'narrow')
Inputs may be any that keep to these rules, and one draw needn't show every extreme that they name: order_map is a permutation of the orders 0 to 511. `obs_lon`: several observations may share a grid point.
All inputs are finite; a program needn't handle non-finite values.
Results may differ from a plain program's by a relative error of at most 0.0057.
Values may be sent and summed in bfloat16 or wider, within the bound.
A program may use at most 256 MiB of HBM per device.

v0:
```python
import math

import jax
import jax.numpy as jnp
from jax import lax
from jax.sharding import PartitionSpec as P

LEVELS = 8


def residual_field(field_rows, flat_index, obs_value, weight_rows):
    picked = jnp.take_along_axis(field_rows, flat_index, axis=1)
    misfit = weight_rows * (picked - obs_value)

    def scatter_row(index_row, value_row):
        return jnp.zeros((field_rows.shape[1],), jnp.float32).at[index_row].add(value_row)

    return jax.vmap(scatter_row)(flat_index, misfit)


def body(
    control, legendre, loc_spectrum, ensemble, order_map, obs_level, obs_lon, obs_value, obs_weight
):
    slot_count = control.shape[0]
    column_count = control.shape[3]
    lat_count = legendre.shape[2]
    lat_local = ensemble.shape[0]
    lon_count = ensemble.shape[2]
    member_local = column_count // LEVELS
    groups = lax.axis_size("wide")
    scaled = (control.astype(jnp.float32) * loc_spectrum[:, None, :, None]).astype(jnp.bfloat16)
    coeff = jnp.einsum("mjb,mcjk->bcmk", legendre, scaled, preferred_element_type=jnp.float32)
    coeff = coeff.astype(jnp.bfloat16).reshape(lat_count, 2 * slot_count, column_count)
    order_grid = order_map.reshape(groups, slot_count)
    longitude = jnp.arange(lon_count, dtype=jnp.int32)
    turns = order_grid[:, :, None] * longitude[None, None, :] % lon_count
    angle = turns.astype(jnp.float32) * (2.0 * math.pi / lon_count)
    factor = jnp.where(order_grid == 0, 1.0, 2.0).astype(jnp.float32)[:, :, None]
    fourier = jnp.stack([factor * jnp.cos(angle), -factor * jnp.sin(angle)], axis=1)
    fourier = fourier.reshape(groups * 2 * slot_count, lon_count).astype(jnp.bfloat16)
    field = jnp.einsum(
        "bsk,so->bko",
        lax.all_to_all(coeff, "wide", split_axis=0, concat_axis=1, tiled=True),
        fourier,
        preferred_element_type=jnp.float32,
    )
    ens_full = ensemble.astype(jnp.float32).reshape(lat_local, member_local, LEVELS, lon_count)
    partial_sum = jnp.sum(
        field.reshape(lat_local, member_local, LEVELS, lon_count) * ens_full, axis=1
    )
    slab_sum = lax.psum_scatter(partial_sum, "narrow", scatter_dimension=1, tiled=True)
    thickness = slab_sum.shape[1]
    slab_start = lax.axis_index("narrow") * thickness
    inside = (obs_level >= slab_start) & (obs_level < slab_start + thickness)
    local_index = jnp.clip(obs_level - slab_start, 0, thickness - 1) * lon_count + obs_lon
    masked_weight = jnp.where(inside, obs_weight, 0.0)
    slab_grad = residual_field(
        slab_sum.reshape(lat_local, thickness * lon_count), local_index, obs_value, masked_weight
    )
    slab_grad = slab_grad.reshape(lat_local, thickness, lon_count)
    obs_grad = lax.all_gather(slab_grad, "narrow", axis=1, tiled=True)
    member_grad = (
        (obs_grad[:, None] * ens_full)
        .reshape(lat_local, column_count, lon_count)
        .astype(jnp.bfloat16)
    )
    backward = jnp.einsum(
        "bko,so->bsk", member_grad, fourier, preferred_element_type=jnp.float32
    ).astype(jnp.bfloat16)
    received = lax.all_to_all(backward, "wide", split_axis=1, concat_axis=0, tiled=True)
    width = received.shape[2]
    blocks = received.reshape(lat_count, 2, slot_count, width)
    adjoint = jnp.einsum("mjb,bcmk->mcjk", legendre, blocks, preferred_element_type=jnp.float32)
    return control.astype(jnp.float32) + loc_spectrum[:, None, :, None] * adjoint


def solution(mesh):
    return jax.shard_map(
        body,
        mesh=mesh,
        in_specs=(
            P("wide", None, None, "narrow"),
            P("wide", None, None),
            P("wide", None),
            P("wide", "narrow", None),
            P(),
            P("wide", None),
            P("wide", None),
            P("wide", None),
            P("wide", None),
        ),
        out_specs=P("wide", None, None, "narrow"),
        check_vma=False,
    )
```

profile of v0, /device:TPU:1, one launch (start us, length us, event | category | flops | bytes accessed | tf_op | source)
XLA Modules:
  0.0 1322.4 jit_solution(10794337426974262754)
XLA Ops:
  6.5 0.0 copy-start
  6.5 22.4 %copy.45 = bf16[64,2,512,128]{2,3,1,0:T(8,128)(2,1)} copy(bf16[64,2,512,128]{3,2,1,0:T(8,128)(2,1)} %param.9) | data formatting | bytes 33554432 | tf_op args[0]
  29.0 0.0 copy-done
  29.0 23.7 %convert_bitcast_fusion.2 = bf16[512,2,64,128]{0,3,1,2:T(8,128)(2,1)} fusion(bf16[64,512,512]{2,1,0:T(8,128)(2,1)} %param.10, bf16[64,2,512,128]{2,3,1,0:T(8,128)(2,1)} %copy.45, f32[64,512]{1,0:T(8,128)S(1)} %copy-done), kind=kOutput, calls=%fused_computation.20 | convolution fusion | flops 8623489024 | bytes 67239936 | tf_op jit(solution)/shard_map/mjb,mcjk->bcmk/dot_general | solution.py:32
  52.6 23.2 %copy.46 = bf16[512,2,64,128]{3,2,1,0:T(8,128)(2,1)} copy(bf16[512,2,64,128]{0,3,1,2:T(8,128)(2,1)} %convert_bitcast_fusion.2) | data formatting | bytes 33554432 | tf_op jit(solution)/shard_map/convert_element_type | solution.py:33
  75.8 0.0 copy-start.6
  75.8 6.5 all-to-all-start
  82.3 0.2 reduce-scatter.2.cloned.1.call-start
  82.5 0.0 copy-done.6
  82.6 0.1 reshape.110
  82.6 9.2 cosine_multiply_fusion
  91.8 0.2 maximum_convert_fusion
  92.0 352.5 %all-to-all-done = bf16[512,128,128]{2,1,0:T(8,128)(2,1)} async-done(((bf16[512,128,128]{2,1,0:T(8,128)(2,1)}), bf16[512,128,128]{2,1,0:T(8,128)(2,1)}, u32[]{:S(2)}, u32[]{:S(2)}) %all-to-all-start) | async-done | bytes 16777248 | tf_op jit(solution)/shard_map/all_to_all | solution.py:43
  444.5 14.1 %copy.47 = bf16[64,8,128,128]{3,2,1,0:T(8,128)(2,1)} copy(bf16[64,8,128,128]{3,2,0,1:T(8,128)(2,1)} %bitcast.8) | data formatting | bytes 33554432 | tf_op jit(solution)/shard_map/all_to_all | solution.py:43
  458.6 22.4 %copy.48 = bf16[64,128,1024]{2,1,0:T(8,128)(2,1)} copy(bf16[64,128,1024]{1,2,0:T(8,128)(2,1)} %bitcast.72) | data formatting | bytes 33554432 | tf_op jit(solution)/shard_map/bsk,so->bko/dot_general | solution.py:41
  481.0 0.0 copy-start.2
  481.0 0.0 copy-start.3
  481.0 0.0 copy-start.8
  481.0 0.0 copy-start.7
  481.0 23.8 %fusion.2 = f32[64,8,1024]{2,1,0:T(8,128)S(1)} fusion(bf16[64,128,1024]{2,1,0:T(8,128)(2,1)} %param.12, bf16[1024,1024,1,1]{1,0,3,2:T(8,128)(2,1)S(1)} %bitcast.74, bf16[64,128,1024]{2,1,0:T(8,128)(2,1)} %copy.48), kind=kOutput, calls=%fused_computation.8 | convolution fusion | flops 17204510720 | bytes 37748736 | tf_op jit(solution)/shard_map/bsk,so->bko/dot_general | solution.py:41
  504.8 2.6 copy.49
  507.3 0.0 reduce-scatter.2.cloned.1.call-update
  507.3 0.0 all-gather.2.cloned.1.call-start
  507.4 0.0 copy-done.2
  507.4 0.0 copy-done.3
  507.5 0.0 copy-done.8
  507.5 0.1 multiply_reduce_fusion
  507.6 0.0 copy-done.7
  507.6 0.1 and_reduce_fusion
  507.8 31.3 %reduce-scatter.2.cloned.1.call-done = f32[64,2,1024]{2,0,1:T(8,128)} async-done(((f32[64,8,1024]{2,0,1:T(8,128)}), f32[64,2,1024]{2,0,1:T(8,128)}) %reduce-scatter.2.cloned.1.call-update) | async-done | bytes 524304 | tf_op jit(solution)/shard_map/reduce_scatter | solution.py:51
  539.1 1.1 copy.61
  540.2 0.0 copy-start.4
  540.2 0.0 copy-start.5
  540.2 129.5 %gather_fusion = f32[16384]{0:T(1024)S(1)} fusion(f32[64,2048]{1,0:T(8,128)S(1)} %bitcast.68, s32[16384]{0:T(1024)S(1)} %bitcast.69), kind=kCustom, calls=%fused_computation | custom fusion | bytes 262144 | tf_op jit(solution)/shard_map/jit(take_along_axis)/gather | solution.py:12
  669.7 0.0 copy-done.4
  669.7 0.0 copy-done.5
  669.7 0.1 multiply_bitcast_fusion
  669.8 87.7 %scatter_custom_fusion = f32[131072]{0:T(1024)S(1)} fusion(s32[16384]{0:T(1024)S(1)} %bitcast.77, f32[16384]{0:T(1024)S(1)} %bitcast.78, f32[]{:T(128)} %constant.24.clone.1), kind=kCustom, calls=%fused_computation.34 | custom fusion | flops 16384 | bytes 524292
  757.5 0.3 reshape.114
  757.8 1.0 copy.51
  758.8 0.0 all-gather.2.cloned.1.call-update
  758.8 36.7 %all-gather.2.cloned.1.call-done = f32[64,8,1024]{2,0,1:T(8,128)} async-done(((f32[64,2,1024]{2,0,1:T(8,128)}), f32[64,8,1024]{2,0,1:T(8,128)}) %all-gather.2.cloned.1.call-update) | async-done | bytes 2097168 | tf_op jit(solution)/shard_map/all_gather | solution.py:61
  795.5 2.8 copy.52
  798.3 22.1 %convert_bitcast_fusion.1 = bf16[64,1024,128]{2,1,0:T(8,128)(2,1)S(1)} fusion(bf16[1024,1024,1]{1,0,2:T(8,128)(2,1)S(1)} %bitcast.75, bf16[64,128,1024]{2,1,0:T(8,128)(2,1)} %param.12, f32[64,8,1024]{2,1,0:T(8,128)S(1)} %copy.52), kind=kOutput, calls=%fused_computation.18 | convolution fusion | flops 17213423616 | bytes 37748736 | tf_op jit(solution)/shard_map/bko,so->bsk/dot_general | solution.py:67
  820.4 36.8 %copy.53 = bf16[64,1024,128]{2,0,1:T(8,128)(2,1)S(1)} copy(bf16[64,1024,128]{2,1,0:T(8,128)(2,1)S(1)} %convert_bitcast_fusion.1) | data formatting | bytes 33554432 | tf_op jit(solution)/shard_map/convert_element_type | solution.py:69
  857.2 367.1 %all_to_all.33 = bf16[64,1024,128]{2,0,1:T(8,128)(2,1)S(1)} all-to-all(bf16[64,1024,128]{2,0,1:T(8,128)(2,1)S(1)} %copy.53), channel_id=1, replica_groups=mesh['wide'=8,'narrow'=4] {'wide'}, dimensions={1} | all-to-all | bytes 33554432 | tf_op jit(solution)/shard_map/all_to_all | solution.py:70
  1224.2 0.0 copy-start.1
  1224.2 11.8 copy.55
  1236.0 0.0 copy-done.1
  1236.0 46.2 %convert_add_fusion = f32[64,2,512,128]{2,3,1,0:T(8,128)} fusion(bf16[64,2,512,128]{2,3,1,0:T(8,128)(2,1)} %copy.45, f32[64,512]{1,0:T(8,128)S(1)} %copy-done.1, bf16[64,512,512]{2,1,0:T(8,128)(2,1)} %param.10, bf16[512,2,64,128]{3,2,1,0:T(8,128)(2,1)} %bitcast.70), kind=kOutput, calls=%fused_computation.4 | convolution fusion | flops 8615100416 | bytes 100794368 | tf_op jit(solution)/shard_map/mjb,bcmk->mcjk/dot_general | solution.py:73
  1282.2 33.4 %copy.57 = f32[64,2,512,128]{3,2,1,0:T(8,128)} copy(f32[64,2,512,128]{2,3,1,0:T(8,128)} %convert_add_fusion) | data formatting | bytes 67108864 | tf_op jit(solution)/shard_map/add | solution.py:74
  (8 shorter events, 0.2 us)
Async XLA Ops:
  6.5 22.4 %copy-start = (f32[64,512]{1,0:T(8,128)S(1)}, f32[64,512]{1,0:T(8,128)}, u32[]{:S(2)}) copy-start(f32[64,512]{1,0:T(8,128)} %param.11) | copy-start | bytes 393220
  75.8 6.7 copy-start.6
  75.8 368.7 %all-to-all-start = ((bf16[512,128,128]{2,1,0:T(8,128)(2,1)}), bf16[512,128,128]{2,1,0:T(8,128)(2,1)}, u32[]{:S(2)}, u32[]{:S(2)}) async-start(bf16[512,128,128]{2,1,0:T(8,128)(2,1)} %bitcast.71), calls=%async_computation | async-start | bytes 33554432 | tf_op jit(solution)/shard_map/all_to_all | solution.py:43
  82.3 456.8 %reduce-scatter.2.cloned.1.call-start = ((), (), s32[]{:S(2)}) async-start(), calls=%async_computation.3 | async-start | bytes 2621440 | tf_op jit(solution)/shard_map/reduce_scatter | solution.py:51
  481.0 26.4 %copy-start.2 = (s32[64,256]{1,0:T(8,128)S(1)}, s32[64,256]{1,0:T(8,128)}, u32[]{:S(2)}) copy-start(s32[64,256]{1,0:T(8,128)} %param.15) | copy-start | bytes 196612
  481.0 26.4 %copy-start.3 = (s32[64,256]{1,0:T(8,128)S(1)}, s32[64,256]{1,0:T(8,128)}, u32[]{:S(2)}) copy-start(s32[64,256]{1,0:T(8,128)} %param.14) | copy-start | bytes 196612
  481.0 26.6 %copy-start.8 = (s32[2]{0:T(128)S(1)}, s32[2]{0:T(128)}, u32[]{:S(2)}) copy-start(s32[2]{0:T(128)} %constant.52) | copy-start | bytes 28
  481.0 26.7 %copy-start.7 = (s32[2]{0:T(128)S(1)}, s32[2]{0:T(128)}, u32[]{:S(2)}) copy-start(s32[2]{0:T(128)} %constant.55) | copy-start | bytes 28
  507.3 288.1 %all-gather.2.cloned.1.call-start = ((), (), s32[]{:S(2)}) async-start(), calls=%async_computation.4 | async-start | bytes 2621440 | tf_op jit(solution)/shard_map/all_gather | solution.py:61
  540.2 129.5 %copy-start.4 = (f32[64,256]{1,0:T(8,128)S(1)}, f32[64,256]{1,0:T(8,128)}, u32[]{:S(2)}) copy-start(f32[64,256]{1,0:T(8,128)} %param.16) | copy-start | bytes 196612
  540.2 129.5 %copy-start.5 = (f32[64,256]{1,0:T(8,128)S(1)}, f32[64,256]{1,0:T(8,128)}, u32[]{:S(2)}) copy-start(f32[64,256]{1,0:T(8,128)} %param.17) | copy-start | bytes 196612
  1224.2 11.8 copy-start.1
Sparse Core Ops, SparseCore 0:
  507.5 31.5 reduce-scatter.1
  758.9 36.5 all-gather.1
where the time goes:
time: 1330 us; the launch traced here: 1320 us
  waiting for transfers between devices  420 us (32%)
  blocking collectives  367 us (28%)
  local copies, waits for them, and re-layouts  301 us (23%)
  matrix products  116 us (9%)
  other arithmetic  97.3 us (7%)
  between operations  13.6 us (1%)
    all_to_all x1, blocking collectives, body(): lax.all_to_all(backward, 'wide', split_axis=1, concat_axis=0, tiled=True)  367 us
    all_to_all x1, waiting for transfers between devices, body(): lax.all_to_all(coeff, 'wide', split_axis=0, concat_axis=1, tiled=True)  352 us
    gather x2, local copies, waits for them, and re-layouts, residual_field(): picked = jnp.take_along_axis(field_rows, flat_index, axis=1)  129 us
    unnamed x6, other arithmetic  88 us
    dot_general x1, matrix products, body(): jnp.einsum('mjb,bcmk->mcjk', legendre, blocks, preferred_element_type=jnp...  46.2 us
    convert_element_type x1, local copies, waits for them, and re-layouts, body(): backward = jnp.einsum('bko,so->bsk', member_grad, fourier, preferred_elem...  36.8 us
    all_gather x1, waiting for transfers between devices, body(): obs_grad = lax.all_gather(slab_grad, 'narrow', axis=1, tiled=True)  36.7 us
    add x1, local copies, waits for them, and re-layouts, body(): control.astype(jnp.float32) + loc_spectrum[:, None, :, None] * adjoint  33.4 us
  transfers between devices with their start and end apart: 3, of which 3 were waited for; matrix products, arithmetic and copies ran while one was open for 1% of the time, Pallas kernels for 0%

commit v1 on v0

v1 whole, which is shorter than its diff:
```python
import functools

import jax
import jax.numpy as jnp
from jax import lax
from jax.experimental import pallas as pl
from jax.experimental.pallas import tpu as pltpu
from jax.sharding import PartitionSpec as P

LEVELS = 8
GROUP = 8
PACK = 16
MIB = 1 << 20

COS = (0.99999921, -19.73898036, 64.92865742, -85.27162153, 58.79049212, -21.07110563)
SIN = (6.28318279, -41.34141938, 81.59613876, -76.57968785, 41.20374363, -12.26885994)


def horner(terms, square):
    total = terms[-1] * square + terms[-2]
    for term in terms[-3::-1]:
        total = total * square + term
    return total


def spread_levels(members, level):
    count, nobs = members.shape
    at_level = lax.broadcasted_iota(jnp.int32, (LEVELS, nobs), 0).astype(jnp.float32) == level
    spread = jnp.where(at_level[None], jnp.broadcast_to(members[:, None], (count, LEVELS, nobs)), 0.0)
    return spread.reshape(count * LEVELS, nobs)


def sample_kernel(lon_ref, level_ref, ens_ref, out_ref):
    rows, columns, lon_count = ens_ref.shape
    nobs = lon_ref.shape[1]
    for row in range(rows):
        hit = lax.broadcasted_iota(jnp.int32, (lon_count, nobs), 0) == lon_ref[row : row + 1, :]
        onehot = jnp.where(hit, 1.0, 0.0).astype(jnp.bfloat16)
        picked = jnp.dot(ens_ref[row], onehot, preferred_element_type=jnp.float32)
        at_level = lax.broadcasted_iota(jnp.int32, (LEVELS, nobs), 0) == level_ref[row : row + 1, :]
        picked = jnp.where(at_level[None], picked.reshape(columns // LEVELS, LEVELS, nobs), 0.0)
        out_ref[row] = jnp.sum(picked, axis=1).astype(jnp.bfloat16)


def split_code(code, lon_count):
    level = jnp.floor((code + 0.5) * (1.0 / lon_count))
    return level, code - level * lon_count


def legendre_kernel(leg_ref, control_ref, loc_ref, out_ref, held):
    orders, _, _, width = control_ref.shape
    lat_count = leg_ref.shape[2]
    part = pl.program_id(1)

    def one(order, carry):
        loc = jnp.broadcast_to(loc_ref[pl.ds(order, 1), :], (width, loc_ref.shape[1])).T
        scaled = [
            (control_ref[order, c].astype(jnp.float32) * loc).astype(jnp.bfloat16) for c in range(2)
        ]
        coeff = lax.dot_general(
            leg_ref[order],
            jnp.concatenate(scaled, axis=1),
            (((0,), (0,)), ((), ())),
            preferred_element_type=jnp.float32,
        )
        for c in range(2):
            held[c, pl.ds(part * orders + order, lat_count, stride=PACK), :] = coeff[
                :, c * width : (c + 1) * width
            ]
        return carry

    lax.fori_loop(0, orders, one, 0, unroll=2)

    @pl.when(part == pl.num_programs(1) - 1)
    def _():
        for c in range(2):
            out_ref[:, c] = held[c].reshape(lat_count, PACK, width).astype(jnp.bfloat16)


def groups_of(rows, work):
    def one(step, carry):
        work(pl.multiple_of(step * GROUP, GROUP))
        return carry

    lax.fori_loop(0, rows // GROUP, one, 0)


def wave_kernel(lon_count, code_ref, freq_ref, factor_ref, wave_ref):
    def work(first):
        _, lons = split_code(code_ref[pl.ds(first, GROUP), :], lon_count)
        for row in range(GROUP):
            turns = freq_ref[...] * lons[row : row + 1, :]
            turns = turns - jnp.round(turns)
            square = turns * turns
            factor = factor_ref[...]
            wave_ref[first + row] = jnp.concatenate(
                [factor * horner(COS, square), -factor * (turns * horner(SIN, square))], axis=0
            ).astype(jnp.bfloat16)

    groups_of(wave_ref.shape[0], work)


def forward_kernel(lon_count, code_ref, members_ref, coeff_ref, wave_ref, picked_ref):
    def work(first):
        levels, _ = split_code(code_ref[pl.ds(first, GROUP), :], lon_count)
        picked = []
        for row in range(GROUP):
            members = members_ref[first + row].astype(jnp.float32)
            spread = spread_levels(members, levels[row : row + 1, :]).astype(jnp.bfloat16)
            weighed = jnp.dot(
                coeff_ref[first + row], spread, preferred_element_type=jnp.float32
            )
            picked.append(
                jnp.sum(wave_ref[first + row].astype(jnp.float32) * weighed, axis=0, keepdims=True)
            )
        picked_ref[pl.ds(first, GROUP), :] = jnp.concatenate(picked, axis=0)

    groups_of(wave_ref.shape[0], work)


def misfit_kernel(
    part_ref, value_ref, weight_ref, out_ref,
    near, mine, far, gathered, final, send_sem, recv_sem,
):
    wide, narrow = part_ref.shape[:2]
    me_wide, me_narrow = lax.axis_index("wide"), lax.axis_index("narrow")

    def narrow_peer(step):
        return (me_wide, lax.rem(me_narrow + step, narrow))

    def wide_peer(step):
        return (lax.rem(me_wide + step, wide), me_narrow)

    peers = [narrow_peer(step) for step in range(1, narrow)]
    peers += [wide_peer(step) for step in range(1, wide)]
    barrier = pltpu.get_barrier_semaphore()
    for peer in peers:
        pl.semaphore_signal(
            barrier, inc=1, device_id=peer, device_id_type=pl.DeviceIdType.MESH
        )
    pl.semaphore_wait(barrier, len(peers))

    used = iter(range(2 * len(peers)))

    def send(source, target, peer):
        slot = next(used)
        copy = pltpu.make_async_remote_copy(
            src_ref=source,
            dst_ref=target,
            send_sem=send_sem.at[slot],
            recv_sem=recv_sem.at[slot],
            device_id=peer,
            device_id_type=pl.DeviceIdType.MESH,
        )
        copy.start()
        return copy

    copies = []
    for step in range(1, narrow):
        peer = narrow_peer(step)
        copies.append(send(part_ref.at[:, peer[1]], near.at[step - 1], peer))
    total = part_ref[:, me_narrow]
    for step, copy in enumerate(copies):
        copy.wait_recv()
        total = total + near[step]
    mine[...] = total

    over_wide = []
    for step in range(1, wide):
        peer = wide_peer(step)
        over_wide.append(send(mine.at[peer[0]], far.at[step - 1], peer))
    total = mine[me_wide]
    for step, copy in enumerate(over_wide):
        copy.wait_recv()
        total = total + far[step]
    gathered[me_wide] = weight_ref[...] * (total - value_ref[...])

    back_wide = [
        send(gathered.at[me_wide], gathered.at[me_wide], wide_peer(step))
        for step in range(1, wide)
    ]
    for copy in back_wide:
        copy.wait_recv()
    back_narrow = [
        send(gathered, final.at[me_narrow], narrow_peer(step)) for step in range(1, narrow)
    ]
    final[me_narrow] = gathered[...]
    for copy in back_narrow:
        copy.wait_recv()
    for group in range(narrow):
        out_ref[:, group] = final[group]
    for copy in copies + over_wide + back_wide + back_narrow:
        copy.wait_send()


def backward_kernel(lon_count, code_ref, members_ref, misfit_ref, wave_ref, back_ref):
    def work(first):
        levels, _ = split_code(code_ref[pl.ds(first, GROUP), :], lon_count)
        misfits = misfit_ref[pl.ds(first, GROUP), :]
        for row in range(GROUP):
            members = members_ref[first + row].astype(jnp.float32) * misfits[row : row + 1, :]
            spread = spread_levels(members, levels[row : row + 1, :]).astype(jnp.bfloat16)
            back_ref[first + row] = lax.dot_general(
                wave_ref[first + row],
                spread,
                (((1,), (1,)), ((), ())),
                preferred_element_type=jnp.float32,
            ).astype(jnp.bfloat16)

    groups_of(wave_ref.shape[0], work)


def adjoint_kernel(leg_ref, control_ref, loc_ref, back_ref, out_ref, held):
    orders, _, _, width = control_ref.shape
    lat_count = leg_ref.shape[2]
    part = pl.program_id(1)

    @pl.when(part == 0)
    def _():
        for c in range(2):
            held[c] = back_ref[:, c].astype(jnp.float32).reshape(lat_count * PACK, width)

    def one(order, carry):
        loc = jnp.broadcast_to(loc_ref[pl.ds(order, 1), :], (width, loc_ref.shape[1])).T
        back = [
            held[c, pl.ds(part * orders + order, lat_count, stride=PACK), :].astype(jnp.bfloat16)
            for c in range(2)
        ]
        adjoint = jnp.dot(
            leg_ref[order], jnp.concatenate(back, axis=1), preferred_element_type=jnp.float32
        )
        for c in range(2):
            out_ref[order, c] = (
                control_ref[order, c].astype(jnp.float32)
                + loc * adjoint[:, c * width : (c + 1) * width]
            )
        return carry

    lax.fori_loop(0, orders, one, 0, unroll=2)


def params(mib):
    return pltpu.CompilerParams(vmem_limit_bytes=mib * MIB)


def body(
    control, legendre, loc_spectrum, ensemble, order_map, obs_level, obs_lon, obs_value, obs_weight
):
    slots, _, degrees, columns = control.shape
    lat_count = legendre.shape[2]
    lat_local, _, lon_count = ensemble.shape
    nobs = obs_lon.shape[1]
    members = columns // LEVELS
    half = PACK // 2
    rows = 32
    wide, narrow = lax.axis_size("wide"), lax.axis_size("narrow")

    code = (obs_level * lon_count + obs_lon).astype(jnp.float32)
    all_code = lax.all_gather(code, "wide", axis=0, tiled=True)

    def by_rows(*shape):
        return pl.BlockSpec((rows,) + shape, lambda i: (i,) + (0,) * len(shape))

    def by_group(*shape):
        return pl.BlockSpec((GROUP,) + shape, lambda i: (i,) + (0,) * len(shape))

    sampled = pl.pallas_call(
        sample_kernel,
        grid=(lat_local // GROUP,),
        in_specs=[by_group(nobs), by_group(nobs), by_group(columns, lon_count)],
        out_specs=by_group(members, nobs),
        out_shape=jax.ShapeDtypeStruct((lat_local, members, nobs), jnp.bfloat16),
        compiler_params=params(32),
        cost_estimate=pl.CostEstimate(
            flops=2 * lat_local * columns * lon_count * nobs,
            bytes_accessed=2 * ensemble.size,
            transcendentals=0,
        ),
        name="sample",
    )(obs_lon, obs_level, ensemble)
    all_sampled = lax.all_gather(sampled, "wide", axis=0, tiled=True)

    leg_spec = pl.BlockSpec((half, degrees, lat_count), lambda i, j: (2 * i + j, 0, 0))
    control_spec = pl.BlockSpec((half, 2, degrees, columns), lambda i, j: (2 * i + j, 0, 0, 0))
    loc_spec = pl.BlockSpec((half, degrees), lambda i, j: (2 * i + j, 0))
    mixed_spec = pl.BlockSpec((lat_count, 2, PACK, columns), lambda i, j: (0, 0, i, 0))
    held = pltpu.VMEM((2, lat_count * PACK, columns), jnp.float32)
    legendre_flops = 4 * slots * degrees * lat_count * columns

    coeff = pl.pallas_call(
        legendre_kernel,
        grid=(slots // PACK, 2),
        in_specs=[leg_spec, control_spec, loc_spec],
        out_specs=mixed_spec,
        out_shape=jax.ShapeDtypeStruct((lat_count, 2, slots, columns), jnp.bfloat16),
        scratch_shapes=[held],
        compiler_params=params(56),
        cost_estimate=pl.CostEstimate(
            flops=legendre_flops,
            bytes_accessed=2 * (legendre.size + 2 * control.size),
            transcendentals=0,
        ),
        name="legendre",
    )(legendre, control, loc_spectrum)
    coeff = coeff.reshape(lat_count, 2 * slots, columns)

    first = lax.axis_index("wide") * slots
    orders = lax.dynamic_slice_in_dim(order_map, first, slots)[:, None]
    freq = jnp.broadcast_to(orders.astype(jnp.float32) / lon_count, (slots, nobs))
    factor = jnp.broadcast_to(jnp.where(orders == 0, 1.0, 2.0).astype(jnp.float32), (slots, nobs))
    whole = pl.BlockSpec((slots, nobs), lambda i: (0, 0))
    wave_shape = (2 * slots, nobs)
    wave = pl.pallas_call(
        functools.partial(wave_kernel, lon_count),
        grid=(lat_count // rows,),
        in_specs=[by_rows(nobs), whole, whole],
        out_specs=by_rows(*wave_shape),
        out_shape=jax.ShapeDtypeStruct((lat_count,) + wave_shape, jnp.bfloat16),
        compiler_params=params(32),
        cost_estimate=pl.CostEstimate(
            flops=40 * lat_count * slots * nobs,
            bytes_accessed=4 * lat_count * slots * nobs,
            transcendentals=0,
        ),
        name="wave",
    )(all_code, freq, factor)
    pair_cost = pl.CostEstimate(
        flops=4 * lat_count * slots * columns * nobs,
        bytes_accessed=4 * lat_count * slots * (columns + nobs),
        transcendentals=0,
    )
    picked = pl.pallas_call(
        functools.partial(forward_kernel, lon_count),
        grid=(lat_count // rows,),
        in_specs=[
            by_rows(nobs),
            by_rows(members, nobs),
            by_rows(2 * slots, columns),
            by_rows(*wave_shape),
        ],
        out_specs=by_rows(nobs),
        out_shape=jax.ShapeDtypeStruct((lat_count, nobs), jnp.float32),
        compiler_params=params(40),
        cost_estimate=pair_cost,
        name="forward",
    )(all_code, all_sampled, coeff, wave)

    owned = lat_local // narrow
    start = lax.axis_index("narrow") * owned
    block = (owned, nobs)
    copies = 2 * (wide + narrow - 2)
    vmem = pl.BlockSpec(memory_space=pltpu.VMEM)
    misfit = pl.pallas_call(
        misfit_kernel,
        in_specs=[vmem] * 3,
        out_specs=vmem,
        out_shape=jax.ShapeDtypeStruct((wide, narrow) + block, jnp.float32),
        scratch_shapes=[
            pltpu.VMEM((narrow - 1, wide) + block, jnp.float32),
            pltpu.VMEM((wide,) + block, jnp.float32),
            pltpu.VMEM((wide - 1,) + block, jnp.float32),
            pltpu.VMEM((wide,) + block, jnp.float32),
            pltpu.VMEM((narrow, wide) + block, jnp.float32),
            pltpu.SemaphoreType.DMA((copies,)),
            pltpu.SemaphoreType.DMA((copies,)),
        ],
        compiler_params=pltpu.CompilerParams(
            collective_id=0, has_side_effects=True, vmem_limit_bytes=24 * MIB
        ),
        name="misfit",
    )(
        picked.reshape((wide, narrow) + block),
        lax.dynamic_slice_in_dim(obs_value, start, owned),
        lax.dynamic_slice_in_dim(obs_weight, start, owned),
    ).reshape(lat_count, nobs)

    back = pl.pallas_call(
        functools.partial(backward_kernel, lon_count),
        grid=(lat_count // rows,),
        in_specs=[
            by_rows(nobs),
            by_rows(members, nobs),
            by_rows(nobs),
            by_rows(*wave_shape),
        ],
        out_specs=by_rows(2 * slots, columns),
        out_shape=jax.ShapeDtypeStruct((lat_count, 2 * slots, columns), jnp.bfloat16),
        compiler_params=params(40),
        cost_estimate=pair_cost,
        name="backward",
    )(all_code, all_sampled, misfit, wave)

    return pl.pallas_call(
        adjoint_kernel,
        grid=(slots // PACK, 2),
        in_specs=[leg_spec, control_spec, loc_spec, mixed_spec],
        out_specs=control_spec,
        out_shape=jax.ShapeDtypeStruct(control.shape, jnp.float32),
        scratch_shapes=[held],
        compiler_params=params(56),
        cost_estimate=pl.CostEstimate(
            flops=legendre_flops,
            bytes_accessed=2 * (legendre.size + 4 * control.size),
            transcendentals=0,
        ),
        name="adjoint",
    )(legendre, control, loc_spectrum, back.reshape(lat_count, 2, slots, columns))


def solution(mesh):
    return jax.shard_map(
        body,
        mesh=mesh,
        in_specs=(
            P("wide", None, None, "narrow"),
            P("wide", None, None),
            P("wide", None),
            P("wide", "narrow", None),
            P(),
            P("wide", None),
            P("wide", None),
            P("wide", None),
            P("wide", None),
        ),
        out_specs=P("wide", None, None, "narrow"),
        check_vma=False,
    )
```

time: 1330 us -> 266 us (0.20)
  waiting for transfers between devices: 420 us -> 0.02 us
  blocking collectives: 367 us -> 27.7 us
  local copies, waits for them, and re-layouts: 301 us -> 10.5 us
  Pallas kernels: 0 us -> 213 us
  matrix products: 116 us -> 0 us
  other arithmetic: 97.3 us -> 0.77 us
    all_to_all x1 -> x0, blocking collectives: 367 us -> none  [body(): lax.all_to_all(backward, 'wide', split_axis=1, concat_axis=0, tiled=True)]
    all_to_all x1 -> x0, waiting for transfers between devices: 352 us -> none  [body(): lax.all_to_all(coeff, 'wide', split_axis=0, concat_axis=1, tiled=True)]
    pallas_call x0 -> x7, Pallas kernels: none -> 213 us  [the longest x1 41.2 us: body(): pl.pallas_call(adjoint_kernel, grid=(slots // PACK, 2), in_specs=[leg_spe...]
    gather x2 -> x0, local copies, waits for them, and re-layouts: 129 us -> none  [residual_field(): picked = jnp.take_along_axis(field_rows, flat_index, axis=1)]
    dot_general x4 -> x0, matrix products: 116 us -> none  [the longest x1 46.2 us: body(): jnp.einsum('mjb,bcmk->mcjk', legendre, blocks, preferred_element_type=jnp...]
    unnamed x6 -> x0, other arithmetic: 88 us -> none
    convert_element_type x2 -> x0, local copies, waits for them, and re-layouts: 60 us -> none  [the longest x1 36.8 us: body(): backward = jnp.einsum('bko,so->bsk', member_grad, fourier, preferred_elem...]
    all_gather x1, waiting for transfers between devices: 36.7 us -> 0.01 us  [body(): all_sampled = lax.all_gather(sampled, 'wide', axis=0, tiled=True)]
  transfers between devices with their start and end apart: 3 -> 1, of which waited for: 3 -> 0; matrix products, arithmetic and copies ran while one was open for 1% -> 1% of each run, Pallas kernels for 0% -> 28%
where the time goes in v1:
time: 266 us; the launch traced here: 265 us
  Pallas kernels  213 us (80%)
  blocking collectives  27.7 us (10%)
  between operations  13.4 us (5%)
  local copies, waits for them, and re-layouts  10.5 us (4%)
    pallas_call x1, Pallas kernels, body(): pl.pallas_call(adjoint_kernel, grid=(slots // PACK, 2), in_specs=[leg_spe...  41.2 us
    pallas_call x1, Pallas kernels, body(): pl.pallas_call(legendre_kernel, grid=(slots // PACK, 2), in_specs=[leg_sp...  39.4 us
    pallas_call x1, Pallas kernels, body(): pl.pallas_call(functools.partial(wave_kernel, lon_count), grid=(lat_count...  34.3 us
    pallas_call x1, Pallas kernels, body(): pl.pallas_call(misfit_kernel, in_specs=[vmem] * 3, out_specs=vmem, out_sh...  31 us
    pallas_call x1, Pallas kernels, body(): pl.pallas_call(functools.partial(backward_kernel, lon_count), grid=(lat_c...  28.8 us
    all_gather x1, blocking collectives, body(): all_code = lax.all_gather(code, 'wide', axis=0, tiled=True)  27.7 us
    pallas_call x1, Pallas kernels, body(): pl.pallas_call(functools.partial(forward_kernel, lon_count), grid=(lat_co...  27.4 us
    pallas_call x1, Pallas kernels, body(): pl.pallas_call(sample_kernel, grid=(lat_local // GROUP,), in_specs=[by_gr...  10.5 us
  transfers between devices with their start and end apart: 1, of which 0 were waited for; matrix products, arithmetic and copies ran while one was open for 1% of the time, Pallas kernels for 28%

profile of v1, /device:TPU:1, one launch (start us, length us, event | category | flops | bytes accessed | tf_op | source)
XLA Modules:
  0.0 265.0 jit_solution(8292622484845193395)
XLA Ops:
  6.5 0.0 all-gather.2.cloned.1.call-start
  6.5 0.0 copy-start
  6.5 5.8 %copy-done = bf16[64,128,1024]{2,1,0:T(8,128)(2,1)S(1)} copy-done((bf16[64,128,1024]{2,1,0:T(8,128)(2,1)S(1)}, bf16[64,128,1024]{2,1,0:T(8,128)(2,1)}, u32[]{:S(2)}) %copy-start) | copy-done | bytes 16777240
  12.3 0.0 copy-start.2
  12.3 0.8 copy-done.2
  13.1 0.0 copy-start.4
  13.1 0.8 copy-done.4
  14.0 0.0 copy-start.3
  14.0 0.0 copy-start.5
  14.0 10.5 %sample.1 = bf16[64,16,256]{2,1,0:T(8,128)(2,1)} custom-call(s32[64,256]{1,0:T(8,128)S(1)} %copy-done.2, s32[64,256]{1,0:T(8,128)S(1)} %copy-done.4, bf16[64,128,1024]{2,1,0:T(8,128)(2,1)S(1)} %copy-done), custom_call_target="tpu_custom_call" | custom-call | flops 4294967296 | bytes 16777216 | tf_op jit(solution)/shard_map/sample/pallas_call | solution.py:267
  24.5 0.0 all-gather.2.cloned.1.call-update
  24.5 0.8 compare_select_fusion
  25.3 0.0 copy-done.3
  25.3 0.0 copy-done.5
  25.3 27.7 %all_gather.6.code_ref = f32[512,256]{1,0:T(8,128)S(1)} all-gather(f32[64,256]{1,0:T(8,128)S(1)} %add_convert_fusion), channel_id=1, replica_groups=mesh['wide'=8,'narrow'=4] {'wide'}, dimensions={0}, use_global_device_ids=true | all-gather | bytes 589824 | tf_op jit(solution)/shard_map/all_gather | solution.py:259
  53.0 0.1 broadcast_in_dim.19.freq_ref
  53.0 0.1 broadcast_in_dim.22.factor_ref
  53.1 34.3 %wave.1.wave_ref = bf16[512,128,256]{2,1,0:T(8,128)(2,1)} custom-call(f32[512,256]{1,0:T(8,128)S(1)} %all_gather.6.code_ref, f32[64,256]{1,0:T(8,128)S(1)} %broadcast_in_dim.19.freq_ref, f32[64,256]{1,0:T(8,128)S(1)} %broadcast_in_dim.22.factor_ref), custom_call_target="tpu_custom_call" | custom-call | flops 335544320 | bytes 33554432 | tf_op jit(solution)/shard_map/wave/pallas_call | solution.py:313
  87.4 0.7 constant_dynamic-slice_fusion
  88.1 39.4 %legendre.1 = bf16[512,2,64,128]{3,2,1,0:T(8,128)(2,1)} custom-call(bf16[64,512,512]{2,1,0:T(8,128)(2,1)} %leg_ref.3, bf16[64,2,512,128]{3,2,1,0:T(8,128)(2,1)} %control_ref.3, f32[64,512]{1,0:T(8,128)} %loc_ref.3), custom_call_target="tpu_custom_call" | custom-call | flops 8589934592 | bytes 67108864 | tf_op jit(solution)/shard_map/legendre/pallas_call | solution.py:290
  127.5 0.0 all-gather.2.cloned.1.call-done.members_ref
  127.5 0.0 copy-start.1
  127.5 2.2 copy-done.1
  129.7 27.4 %forward.1 = f32[512,256]{1,0:T(8,128)S(1)} custom-call(f32[512,256]{1,0:T(8,128)S(1)} %all_gather.6.code_ref, bf16[512,16,256]{2,1,0:T(8,128)(2,1)S(1)} %copy-done.1, bf16[512,128,128]{2,1,0:T(8,128)(2,1)} %bitcast.6, bf16[512,128,256]{2,1,0:T(8,128)(2,1)} %wave.1.wave_ref), custom_call_target="tpu_custom_call" | custom-call | flops 4294967296 | bytes 50331648 | tf_op jit(solution)/shard_map/forward/pallas_call | solution.py:332
  157.1 31.0 %misfit.1 = f32[8,4,16,256]{3,2,1,0:T(8,128)S(1)} custom-call(f32[8,4,16,256]{3,2,1,0:T(8,128)S(1)} %bitcast.5, f32[16,256]{1,0:T(8,128)S(1)} %get-tuple-element.8.value_ref, f32[16,256]{1,0:T(8,128)S(1)} %get-tuple-element.7.weight_ref), custom_call_target="tpu_custom_call" | custom-call | tf_op jit(solution)/shard_map/misfit/pallas_call | solution.py:353
  188.1 28.8 %backward.1 = bf16[512,128,128]{2,1,0:T(8,128)(2,1)} custom-call(f32[512,256]{1,0:T(8,128)S(1)} %all_gather.6.code_ref, bf16[512,16,256]{2,1,0:T(8,128)(2,1)S(1)} %copy-done.1, f32[512,256]{1,0:T(8,128)S(1)} %bitcast.4, bf16[512,128,256]{2,1,0:T(8,128)(2,1)} %wave.1.wave_ref), custom_call_target="tpu_custom_call" | custom-call | flops 4294967296 | bytes 50331648 | tf_op jit(solution)/shard_map/backward/pallas_call | solution.py:377
  216.9 41.2 %adjoint.1 = f32[64,2,512,128]{3,2,1,0:T(8,128)} custom-call(bf16[64,512,512]{2,1,0:T(8,128)(2,1)} %leg_ref.3, bf16[64,2,512,128]{3,2,1,0:T(8,128)(2,1)} %control_ref.3, f32[64,512]{1,0:T(8,128)} %loc_ref.3, bf16[512,2,64,128]{3,2,1,0:T(8,128)(2,1)} %bitcast.7), custom_call_target="tpu_custom_call" | custom-call | flops 8589934592 | bytes 100663296 | tf_op jit(solution)/shard_map/adjoint/pallas_call | solution.py:393
  (1 shorter events, 0.0 us)
Async XLA Ops:
  6.5 120.9 %all-gather.2.cloned.1.call-start = ((), (), s32[]{:S(2)}) async-start(), calls=%async_computation | async-start | bytes 4718592 | tf_op jit(solution)/shard_map/all_gather | solution.py:281
  6.5 5.8 %copy-start = (bf16[64,128,1024]{2,1,0:T(8,128)(2,1)S(1)}, bf16[64,128,1024]{2,1,0:T(8,128)(2,1)}, u32[]{:S(2)}) copy-start(bf16[64,128,1024]{2,1,0:T(8,128)(2,1)} %ens_ref.1) | copy-start | bytes 50331652
  12.3 0.8 copy-start.2
  13.1 0.8 copy-start.4
  14.0 11.3 %copy-start.3 = (s32[64,256]{1,0:T(8,128)S(1)}, s32[64,256]{1,0:T(8,128)}, u32[]{:S(2)}) copy-start(s32[64,256]{1,0:T(8,128)} %lon_ref.1) | copy-start | bytes 196612
  14.0 11.3 %copy-start.5 = (s32[64,256]{1,0:T(8,128)S(1)}, s32[64,256]{1,0:T(8,128)}, u32[]{:S(2)}) copy-start(s32[64,256]{1,0:T(8,128)} %level_ref.1) | copy-start | bytes 196612
  127.5 2.2 copy-start.1
Sparse Core Ops, SparseCore 0:
  24.6 77.4 all-gather.1

commit v2 on v1

--- a/solution.py
+++ b/solution.py
@@ -13,7 +13,7 @@
 MIB = 1 << 20
 
 COS = (0.99999921, -19.73898036, 64.92865742, -85.27162153, 58.79049212, -21.07110563)
-SIN = (6.28318279, -41.34141938, 81.59613876, -76.57968785, 41.20374363, -12.26885994)
+SIN = (-6.28305409, 41.33112295, -81.36549857, 74.47097755, -32.7689024)
 
 
 def horner(terms, square):
@@ -69,7 +69,7 @@
             ]
         return carry
 
-    lax.fori_loop(0, orders, one, 0, unroll=2)
+    lax.fori_loop(0, orders, one, 0, unroll=4)
 
     @pl.when(part == pl.num_programs(1) - 1)
     def _():
@@ -94,7 +94,7 @@
             square = turns * turns
             factor = factor_ref[...]
             wave_ref[first + row] = jnp.concatenate(
-                [factor * horner(COS, square), -factor * (turns * horner(SIN, square))], axis=0
+                [factor * horner(COS, square), factor * (turns * horner(SIN, square))], axis=0
             ).astype(jnp.bfloat16)
 
     groups_of(wave_ref.shape[0], work)
@@ -193,6 +193,36 @@
         copy.wait_send()
 
 
+def share_kernel(own_ref, out_ref, landed, send_sem, recv_sem):
+    wide = out_ref.shape[0]
+    me_wide, me_narrow = lax.axis_index("wide"), lax.axis_index("narrow")
+    peers = [(lax.rem(me_wide + step, wide), me_narrow) for step in range(1, wide)]
+    barrier = pltpu.get_barrier_semaphore()
+    for peer in peers:
+        pl.semaphore_signal(
+            barrier, inc=1, device_id=peer, device_id_type=pl.DeviceIdType.MESH
+        )
+    pl.semaphore_wait(barrier, len(peers))
+    copies = []
+    for slot, peer in enumerate(peers):
+        copy = pltpu.make_async_remote_copy(
+            src_ref=own_ref,
+            dst_ref=landed.at[me_wide],
+            send_sem=send_sem.at[slot],
+            recv_sem=recv_sem.at[slot],
+            device_id=peer,
+            device_id_type=pl.DeviceIdType.MESH,
+        )
+        copy.start()
+        copies.append(copy)
+    landed[me_wide] = own_ref[...]
+    for copy in copies:
+        copy.wait_recv()
+    out_ref[...] = landed[...]
+    for copy in copies:
+        copy.wait_send()
+
+
 def backward_kernel(lon_count, code_ref, members_ref, misfit_ref, wave_ref, back_ref):
     def work(first):
         levels, _ = split_code(code_ref[pl.ds(first, GROUP), :], lon_count)
@@ -236,7 +266,7 @@
             )
         return carry
 
-    lax.fori_loop(0, orders, one, 0, unroll=2)
+    lax.fori_loop(0, orders, one, 0, unroll=4)
 
 
 def params(mib):
@@ -256,7 +286,22 @@
     wide, narrow = lax.axis_size("wide"), lax.axis_size("narrow")
 
     code = (obs_level * lon_count + obs_lon).astype(jnp.float32)
-    all_code = lax.all_gather(code, "wide", axis=0, tiled=True)
+    vmem = pl.BlockSpec(memory_space=pltpu.VMEM)
+    all_code = pl.pallas_call(
+        share_kernel,
+        in_specs=[vmem],
+        out_specs=vmem,
+        out_shape=jax.ShapeDtypeStruct((wide,) + code.shape, jnp.float32),
+        scratch_shapes=[
+            pltpu.VMEM((wide,) + code.shape, jnp.float32),
+            pltpu.SemaphoreType.DMA((wide - 1,)),
+            pltpu.SemaphoreType.DMA((wide - 1,)),
+        ],
+        compiler_params=pltpu.CompilerParams(
+            collective_id=1, has_side_effects=True, vmem_limit_bytes=24 * MIB
+        ),
+        name="share",
+    )(code).reshape(lat_count, nobs)
 
     def by_rows(*shape):
         return pl.BlockSpec((rows,) + shape, lambda i: (i,) + (0,) * len(shape))
@@ -270,7 +315,7 @@
         in_specs=[by_group(nobs), by_group(nobs), by_group(columns, lon_count)],
         out_specs=by_group(members, nobs),
         out_shape=jax.ShapeDtypeStruct((lat_local, members, nobs), jnp.bfloat16),
-        compiler_params=params(32),
+        compiler_params=params(56),
         cost_estimate=pl.CostEstimate(
             flops=2 * lat_local * columns * lon_count * nobs,
             bytes_accessed=2 * ensemble.size,
@@ -349,7 +394,6 @@
     start = lax.axis_index("narrow") * owned
     block = (owned, nobs)
     copies = 2 * (wide + narrow - 2)
-    vmem = pl.BlockSpec(memory_space=pltpu.VMEM)
     misfit = pl.pallas_call(
         misfit_kernel,
         in_specs=[vmem] * 3,

time: 266 us -> 246 us (0.925)
  blocking collectives: 27.7 us -> 0 us
  Pallas kernels: 213 us -> 227 us
  local copies, waits for them, and re-layouts: 10.5 us -> 3.08 us
    all_gather x1 -> x0, blocking collectives: 27.7 us -> none  [body(): all_code = lax.all_gather(code, 'wide', axis=0, tiled=True)]
    pallas_call x0 -> x1, Pallas kernels: none -> 14.5 us  [body(): pl.pallas_call(share_kernel, in_specs=[vmem], out_specs=vmem, out_shape=j...]
    unnamed x12 -> x6, local copies, waits for them, and re-layouts: 9.64 us -> 2.2 us
    pallas_call x1, Pallas kernels: 31 us -> 35.7 us  [body(): pl.pallas_call(misfit_kernel, in_specs=[vmem] * 3, out_specs=vmem, out_sh...]
    pallas_call x1, Pallas kernels: 34.3 us -> 31.1 us  [body(): pl.pallas_call(functools.partial(wave_kernel, lon_count), grid=(lat_count...]
    pallas_call x1, Pallas kernels: 10.5 us -> 13.6 us  [body(): pl.pallas_call(sample_kernel, grid=(lat_local // GROUP,), in_specs=[by_gr...]
    pallas_call x1, Pallas kernels: 39.4 us -> 36.2 us  [body(): pl.pallas_call(legendre_kernel, grid=(slots // PACK, 2), in_specs=[leg_sp...]
  transfers between devices with their start and end apart: 1 -> 1, of which waited for: 0 -> 0; matrix products, arithmetic and copies ran while one was open for 1% -> 1% of each run, Pallas kernels for 28% -> 33%
where the time goes in v2:
time: 246 us; the launch traced here: 245 us
  Pallas kernels  227 us (92%)
  between operations  13.4 us (5%)
  local copies, waits for them, and re-layouts  3.08 us (1%)
    pallas_call x1, Pallas kernels, body(): pl.pallas_call(adjoint_kernel, grid=(slots // PACK, 2), in_specs=[leg_spe...  39.9 us
    pallas_call x1, Pallas kernels, body(): pl.pallas_call(legendre_kernel, grid=(slots // PACK, 2), in_specs=[leg_sp...  36.2 us
    pallas_call x1, Pallas kernels, body(): pl.pallas_call(misfit_kernel, in_specs=[vmem] * 3, out_specs=vmem, out_sh...  35.7 us
    pallas_call x1, Pallas kernels, body(): pl.pallas_call(functools.partial(wave_kernel, lon_count), grid=(lat_count...  31.1 us
    pallas_call x1, Pallas kernels, body(): pl.pallas_call(functools.partial(backward_kernel, lon_count), grid=(lat_c...  28.8 us
    pallas_call x1, Pallas kernels, body(): pl.pallas_call(functools.partial(forward_kernel, lon_count), grid=(lat_co...  27.4 us
    pallas_call x1, Pallas kernels, body(): pl.pallas_call(share_kernel, in_specs=[vmem], out_specs=vmem, out_shape=j...  14.5 us
    pallas_call x1, Pallas kernels, body(): pl.pallas_call(sample_kernel, grid=(lat_local // GROUP,), in_specs=[by_gr...  13.6 us
  transfers between devices with their start and end apart: 1, of which 0 were waited for; matrix products, arithmetic and copies ran while one was open for 1% of the time, Pallas kernels for 33%

profile of v2, /device:TPU:1, one launch (start us, length us, event | category | flops | bytes accessed | tf_op | source)
XLA Modules:
  0.0 244.5 jit_solution(18193701567953135735)
XLA Ops:
  6.5 0.0 copy-start.2
  6.5 0.0 copy-start.1
  6.5 0.0 all-gather.2.cloned.1.call-start
  6.5 13.6 %sample.1 = bf16[64,16,256]{2,1,0:T(8,128)(2,1)} custom-call(s32[64,256]{1,0:T(8,128)} %lon_ref.1, s32[64,256]{1,0:T(8,128)} %level_ref.1, bf16[64,128,1024]{2,1,0:T(8,128)(2,1)} %ens_ref.1), custom_call_target="tpu_custom_call" | custom-call | flops 4294967296 | bytes 16777216 | tf_op jit(solution)/shard_map/sample/pallas_call | solution.py:312
  20.2 0.0 all-gather.2.cloned.1.call-update
  20.2 0.0 copy-done.2
  20.2 0.0 copy-done.1
  20.3 14.5 %share.1 = f32[8,64,256]{2,1,0:T(8,128)S(1)} custom-call(f32[64,256]{1,0:T(8,128)S(1)} %add_convert_fusion.own_ref), custom_call_target="tpu_custom_call" | custom-call | tf_op jit(solution)/shard_map/share/pallas_call | solution.py:290
  34.8 0.8 compare_select_fusion
  35.6 0.1 broadcast_in_dim.19.freq_ref
  35.6 0.1 broadcast_in_dim.22.factor_ref
  35.7 31.1 %wave.1.wave_ref = bf16[512,128,256]{2,1,0:T(8,128)(2,1)} custom-call(f32[512,256]{1,0:T(8,128)S(1)} %bitcast.5, f32[64,256]{1,0:T(8,128)S(1)} %broadcast_in_dim.19.freq_ref, f32[64,256]{1,0:T(8,128)S(1)} %broadcast_in_dim.22.factor_ref), custom_call_target="tpu_custom_call" | custom-call | flops 335544320 | bytes 33554432 | tf_op jit(solution)/shard_map/wave/pallas_call | solution.py:358
  66.8 0.7 constant_dynamic-slice_fusion
  67.5 36.2 %legendre.1 = bf16[512,2,64,128]{3,2,1,0:T(8,128)(2,1)} custom-call(bf16[64,512,512]{2,1,0:T(8,128)(2,1)} %leg_ref.3, bf16[64,2,512,128]{3,2,1,0:T(8,128)(2,1)} %control_ref.3, f32[64,512]{1,0:T(8,128)} %loc_ref.3), custom_call_target="tpu_custom_call" | custom-call | flops 8589934592 | bytes 67108864 | tf_op jit(solution)/shard_map/legendre/pallas_call | solution.py:335
  103.8 0.0 all-gather.2.cloned.1.call-done.members_ref
  103.8 0.0 copy-start
  103.8 2.2 copy-done
  105.9 27.4 %forward.1 = f32[512,256]{1,0:T(8,128)S(1)} custom-call(f32[512,256]{1,0:T(8,128)S(1)} %bitcast.6, bf16[512,16,256]{2,1,0:T(8,128)(2,1)S(1)} %copy-done, bf16[512,128,128]{2,1,0:T(8,128)(2,1)} %bitcast.10, bf16[512,128,256]{2,1,0:T(8,128)(2,1)} %wave.1.wave_ref), custom_call_target="tpu_custom_call" | custom-call | flops 4294967296 | bytes 50331648 | tf_op jit(solution)/shard_map/forward/pallas_call | solution.py:377
  133.3 35.7 %misfit.1 = f32[8,4,16,256]{3,2,1,0:T(8,128)S(1)} custom-call(f32[8,4,16,256]{3,2,1,0:T(8,128)S(1)} %bitcast.9, f32[16,256]{1,0:T(8,128)S(1)} %get-tuple-element.8.value_ref, f32[16,256]{1,0:T(8,128)S(1)} %get-tuple-element.7.weight_ref), custom_call_target="tpu_custom_call" | custom-call | tf_op jit(solution)/shard_map/misfit/pallas_call | solution.py:397
  169.1 28.8 %backward.1 = bf16[512,128,128]{2,1,0:T(8,128)(2,1)} custom-call(f32[512,256]{1,0:T(8,128)S(1)} %bitcast.7, bf16[512,16,256]{2,1,0:T(8,128)(2,1)S(1)} %copy-done, f32[512,256]{1,0:T(8,128)S(1)} %bitcast.8, bf16[512,128,256]{2,1,0:T(8,128)(2,1)} %wave.1.wave_ref), custom_call_target="tpu_custom_call" | custom-call | flops 4294967296 | bytes 50331648 | tf_op jit(solution)/shard_map/backward/pallas_call | solution.py:421
  197.8 39.9 %adjoint.1 = f32[64,2,512,128]{3,2,1,0:T(8,128)} custom-call(bf16[64,512,512]{2,1,0:T(8,128)(2,1)} %leg_ref.3, bf16[64,2,512,128]{3,2,1,0:T(8,128)(2,1)} %control_ref.3, f32[64,512]{1,0:T(8,128)} %loc_ref.3, bf16[512,2,64,128]{3,2,1,0:T(8,128)(2,1)} %bitcast.11), custom_call_target="tpu_custom_call" | custom-call | flops 8589934592 | bytes 100663296 | tf_op jit(solution)/shard_map/adjoint/pallas_call | solution.py:437
  (1 shorter events, 0.0 us)
Async XLA Ops:
  6.5 13.7 %copy-start.2 = (s32[64,256]{1,0:T(8,128)S(1)}, s32[64,256]{1,0:T(8,128)}, u32[]{:S(2)}) copy-start(s32[64,256]{1,0:T(8,128)} %level_ref.1) | copy-start | bytes 196612
  6.5 13.7 %copy-start.1 = (s32[64,256]{1,0:T(8,128)S(1)}, s32[64,256]{1,0:T(8,128)}, u32[]{:S(2)}) copy-start(s32[64,256]{1,0:T(8,128)} %lon_ref.1) | copy-start | bytes 196612
  6.5 97.2 %all-gather.2.cloned.1.call-start = ((), (), s32[]{:S(2)}) async-start(), calls=%async_computation | async-start | bytes 4718592 | tf_op jit(solution)/shard_map/all_gather | solution.py:326
  103.8 2.2 copy-start
Sparse Core Ops, SparseCore 0:
  20.3 77.7 all-gather.1
